TPU v7x, 128 devices: a whole 4x4x4 slice. The times are simulated.
128 devices in a mesh: row: 4 (over x), col: 32 (over y, z, core).
Axes of the slice: x: 4, y: 4, z: 4, core: 2. Of those that a mesh axis runs over, the one named last changes fastest.
Arguments:
- pair_slab: bfloat16 [32, 4096, 128], P('row', 'col'), may hold values from -6 to 6
- pair_bias: bfloat16 [4, 4096, 4096], P(None, 'col', 'row'), may hold values from -5 to 240
- tile_mask: int32 [64, 64], replicated, may hold values from 0 to 1, as said below
- w_proj: bfloat16 [128, 512], replicated, may hold values from -0.5 to 0.5
- w_out: bfloat16 [128, 128], replicated, may hold values from -0.5 to 0.5
- d_out: bfloat16 [32, 4096, 128], P('row', 'col'), may hold values from -6 to 6
Outputs:
- attn_out: bfloat16 [32, 4096, 128], P('row', 'col')
- slab_grads: bfloat16 [32, 4096, 128], P('row', 'col')
- bias_grads: float32 [4096, 4, 4096], P(('row', 'col'))
Inputs may be any that keep to these rules, and one draw needn't show every extreme that they name: tile_mask[a, a] is 1 for every tile a, and tile_mask[a, b] is 0 wherever b > a.
All inputs are finite; a program needn't handle non-finite values.
Results may differ from a plain program's by a relative error of at most 0.019.
Values may be sent and summed in bfloat16 or wider, within the bound.
A program may use at most 192 MiB of HBM per device.

v0:
```python
import jax
import jax.numpy as jnp
from jax import lax
from jax.sharding import PartitionSpec as P

H = 4
DH = 32
TILE = 64
eps_norm = 1e-05
neg_big = -1e30


def normalize(pair_slab):
    entries = pair_slab.astype(jnp.float32)
    centred = entries - jnp.mean(entries, axis=-1, keepdims=True)
    spread = jnp.mean(centred * centred, axis=-1, keepdims=True)
    return centred * lax.rsqrt(spread + eps_norm)


def expand_tiles(tile_block):
    grown = jnp.repeat(jnp.repeat(tile_block, TILE, axis=0), TILE, axis=1)
    return (grown > 0)[None, None]


def pair_scores(query_heads, key_heads, bias_block):
    scores = jnp.einsum(
        "rjhd,rkhd->rhjk", query_heads, key_heads, preferred_element_type=jnp.float32
    )
    return scores + bias_block[None].astype(jnp.float32)


def on_device(pair_slab, pair_bias, tile_mask, w_proj, w_out, d_out):
    row_count, col_count, channels = pair_slab.shape
    head_width = H * DH
    q_scale = DH ** (-0.5)
    own_start = lax.axis_index("col") * col_count
    normed_f, norm_pull = jax.vjp(normalize, pair_slab)
    normed = normed_f.astype(jnp.bfloat16)
    flat_normed = normed.reshape(row_count * col_count, channels)
    w_query = w_proj[:, :head_width]
    w_pair = w_proj[:, head_width : 3 * head_width]
    w_gate = w_proj[:, 3 * head_width :]
    w_pair_back = jnp.transpose(w_pair).astype(jnp.float32)
    queries = (jnp.dot(flat_normed, w_query, preferred_element_type=jnp.float32) * q_scale).astype(
        jnp.bfloat16
    )
    query_heads = queries.reshape(row_count, col_count, H, DH)
    gating = jax.nn.sigmoid(jnp.dot(flat_normed, w_gate, preferred_element_type=jnp.float32))
    gating = gating.reshape(row_count, col_count, head_width)
    bias_rows = lax.all_gather(pair_bias, "row", axis=2, tiled=True)
    gathered_slab = lax.all_gather(normed, "col", axis=1, tiled=True)
    key_values = jnp.dot(
        gathered_slab.reshape(-1, channels), w_pair, preferred_element_type=jnp.float32
    )
    key_values = key_values.astype(jnp.bfloat16).reshape(row_count, -1, 2 * head_width)
    total_cols = key_values.shape[1]
    block_len = min(512, total_cols)
    block_count = total_cols // block_len
    block_ids = jnp.arange(block_count, dtype=jnp.int32)

    def key_slices(block_index):
        key_start = block_index * block_len
        chosen = lax.dynamic_slice_in_dim(key_values, key_start, block_len, 1)
        key_heads = chosen[..., :head_width].reshape(row_count, block_len, H, DH)
        value_heads = chosen[..., head_width:].reshape(row_count, block_len, H, DH)
        bias_block = lax.dynamic_slice_in_dim(bias_rows, key_start, block_len, 2)
        tile_block = lax.dynamic_slice(
            tile_mask,
            (own_start // TILE, key_start // TILE),
            (col_count // TILE, block_len // TILE),
        )
        return (key_heads, value_heads, bias_block, tile_block)

    def stats_step(carried, block_index):
        key_heads, value_heads, bias_block, tile_block = key_slices(block_index)

        def stats_live(running):
            running_max, running_sum = running
            active = expand_tiles(tile_block)
            scores = jnp.where(active, pair_scores(query_heads, key_heads, bias_block), neg_big)
            new_max = jnp.maximum(running_max, jnp.max(scores, axis=-1))
            exp_terms = jnp.where(active, jnp.exp(scores - new_max[..., None]), 0.0)
            return (
                new_max,
                running_sum * jnp.exp(running_max - new_max) + jnp.sum(exp_terms, axis=-1),
            )

        return (
            lax.cond(jnp.any(tile_block > 0), stats_live, lambda unchanged: unchanged, carried),
            None,
        )

    start_max = jnp.full((row_count, H, col_count), neg_big, jnp.float32)
    start_sum = jnp.zeros((row_count, H, col_count), jnp.float32)
    (top_score, exp_total), _ = lax.scan(stats_step, (start_max, start_sum), block_ids)
    log_norm = top_score + jnp.log(exp_total)

    def value_step(carried, block_index):
        key_heads, value_heads, bias_block, tile_block = key_slices(block_index)

        def value_live(value_acc):
            active = expand_tiles(tile_block)
            scores = pair_scores(query_heads, key_heads, bias_block)
            weights = jnp.where(active, jnp.exp(scores - log_norm[..., None]), 0.0).astype(
                jnp.bfloat16
            )
            return value_acc + jnp.einsum(
                "rhjk,rkhd->rjhd", weights, value_heads, preferred_element_type=jnp.float32
            )

        return (
            lax.cond(jnp.any(tile_block > 0), value_live, lambda unchanged: unchanged, carried),
            None,
        )

    value_acc, _ = lax.scan(
        value_step, jnp.zeros((row_count, col_count, H, DH), jnp.float32), block_ids
    )
    attended = value_acc.reshape(row_count, col_count, head_width)
    gated = (gating * attended).astype(jnp.bfloat16)
    attn_out = jnp.dot(gated.reshape(-1, head_width), w_out, preferred_element_type=jnp.float32)
    attn_out = attn_out.astype(jnp.bfloat16).reshape(row_count, col_count, channels)
    d_gated = jnp.dot(
        d_out.reshape(-1, channels), jnp.transpose(w_out), preferred_element_type=jnp.float32
    )
    d_gated = d_gated.reshape(row_count, col_count, head_width)
    d_attended = (d_gated * gating).astype(jnp.bfloat16)
    d_gate_lin = d_gated * attended * gating * (1.0 - gating)
    row_delta = jnp.sum(
        (d_attended.astype(jnp.float32) * attended).reshape(row_count, col_count, H, DH), axis=-1
    )
    row_delta = jnp.transpose(row_delta, (0, 2, 1))
    d_att_heads = d_attended.reshape(row_count, col_count, H, DH)

    def grad_step(carried, block_index):
        key_heads, value_heads, bias_block, tile_block = key_slices(block_index)

        def grad_live(d_query_acc):
            active = expand_tiles(tile_block)
            scores = pair_scores(query_heads, key_heads, bias_block)
            probs = jnp.where(active, jnp.exp(scores - log_norm[..., None]), 0.0)
            weights = probs.astype(jnp.bfloat16)
            d_probs = jnp.einsum(
                "rjhd,rkhd->rhjk", d_att_heads, value_heads, preferred_element_type=jnp.float32
            )
            d_scores = probs * (d_probs - row_delta[..., None])
            d_scores_b = d_scores.astype(jnp.bfloat16)
            d_query_acc = d_query_acc + jnp.einsum(
                "rhjk,rkhd->rjhd", d_scores_b, key_heads, preferred_element_type=jnp.float32
            )
            bias_term = jnp.einsum("rhjk->khj", d_scores)
            d_keys = jnp.einsum(
                "rhjk,rjhd->krhd", d_scores_b, query_heads, preferred_element_type=jnp.float32
            )
            d_values = jnp.einsum(
                "rhjk,rjhd->krhd", weights, d_att_heads, preferred_element_type=jnp.float32
            )
            pair_term = jnp.concatenate(
                [
                    d_keys.reshape(block_len, row_count, head_width),
                    d_values.reshape(block_len, row_count, head_width),
                ],
                axis=-1,
            )
            pair_term = jnp.dot(
                pair_term.reshape(block_len * row_count, 2 * head_width),
                w_pair_back,
                precision=lax.Precision.HIGHEST,
            )
            pair_term = pair_term.reshape(block_len, row_count, channels)
            return (d_query_acc, (bias_term, pair_term))

        def skipped(d_query_acc):
            bias_zero = jnp.zeros((block_len, H, col_count), jnp.float32)
            pair_zero = jnp.zeros((block_len, row_count, channels), jnp.float32)
            return (d_query_acc, (bias_zero, pair_zero))

        return lax.cond(jnp.any(tile_block > 0), grad_live, skipped, carried)

    d_query_acc, block_terms = lax.scan(
        grad_step, jnp.zeros((row_count, col_count, H, DH), jnp.float32), block_ids
    )
    bias_terms = block_terms[0].reshape(total_cols, H, col_count)
    pair_terms = block_terms[1].reshape(total_cols, row_count, channels)
    pair_sum = lax.psum_scatter(
        pair_terms.astype(jnp.bfloat16), "col", scatter_dimension=0, tiled=True
    ).astype(jnp.float32)
    pair_back = jnp.transpose(pair_sum, (1, 0, 2)).reshape(-1, channels)
    d_qg = jnp.concatenate(
        [
            d_query_acc.reshape(row_count * col_count, head_width) * q_scale,
            d_gate_lin.reshape(row_count * col_count, head_width),
        ],
        axis=-1,
    ).astype(jnp.bfloat16)
    w_qg_back = jnp.transpose(jnp.concatenate([w_query, w_gate], axis=1))
    d_normed = jnp.dot(d_qg, w_qg_back, preferred_element_type=jnp.float32) + pair_back
    slab_grads = norm_pull(d_normed.reshape(row_count, col_count, channels))[0]
    partial_sum = lax.psum_scatter(
        bias_terms.astype(jnp.bfloat16), "row", scatter_dimension=0, tiled=True
    ).astype(jnp.float32)
    bias_grads = lax.all_to_all(
        partial_sum.astype(jnp.bfloat16), "col", split_axis=0, concat_axis=2, tiled=True
    ).astype(partial_sum.dtype)
    return (attn_out, slab_grads, bias_grads)


def solution(mesh):
    in_specs = (P("row", "col", None), P(None, "col", "row"), P(), P(), P(), P("row", "col", None))
    out_specs = (P("row", "col", None), P("row", "col", None), P(("row", "col"), None, None))
    return jax.shard_map(
        on_device, mesh=mesh, in_specs=in_specs, out_specs=out_specs, check_vma=False
    )
```

profile of v0, /device:TPU:0, one launch (start us, length us, event | category | flops | bytes accessed | tf_op | source)
XLA Modules:
  0.0 813.9 jit_solution(17003910610374804841)
XLA Ops:
  10.9 2.0 fusion.54
  13.0 2.3 copy.97
  21.4 47.3 %all-gather.3.cloned.1.call-done = bf16[8,4096,128]{2,1,0:T(8,128)(2,1)} async-done(((bf16[8,128,128]{2,1,0:T(8,128)(2,1)}), bf16[8,4096,128]{2,1,0:T(8,128)(2,1)}) %all-gather.3.cloned.1.call-update) | async-done | bytes 8388624 | tf_op jit(solution)/shard_map/all_gather | solution.py:51
  68.6 14.5 %convolution_convert_fusion = bf16[32768,256]{1,0:T(8,128)(2,1)} fusion(bf16[32768,128]{1,0:T(8,128)(2,1)} %bitcast.185, bf16[128,512]{1,0:T(8,128)(2,1)S(1)} %copy-done.10), kind=kOutput, calls=%fused_computation.54 | convolution fusion | flops 2155872256 | bytes 25231360 | tf_op jit(solution)/shard_map/dot_general | solution.py:52
  83.2 21.3 %copy.102 = bf16[8,4096,256]{1,2,0:T(8,128)(2,1)} copy(bf16[8,4096,256]{2,1,0:T(8,128)(2,1)} %bitcast.178) | data formatting | bytes 33554432 | tf_op jit(solution)/shard_map/while | solution.py:116
  104.4 14.2 %all-gather.5.cloned.1.call-done = bf16[4,128,4096]{1,2,0:T(8,128)(2,1)} async-done(((bf16[4,128,1024]{1,2,0:T(8,128)(2,1)}), bf16[4,128,4096]{1,2,0:T(8,128)(2,1)}) %all-gather.5.cloned.1.call-update) | async-done | bytes 4194320 | tf_op jit(solution)/shard_map/all_gather | solution.py:50
  118.7 36.1 %while.51 = (s32[]{:T(128)}, f32[8,4,128]{2,1,0:T(4,128)S(1)}, f32[8,4,128]{2,1,0:T(4,128)S(1)}, s32[8]{0:T(128)S(1)}, s32[64,64]{0,1:T(8,128)}, /*index=5*/s32[...) while((s32[]{:T(128)}, f32[8,4,128]{2,1,0:T(4,128)S(1)}, ...), condition=%wide.region_8.9_spmd, body=%wide.region_2.8_spmd.sunk | while | flops 151265344 | bytes 24269540 | solution.py:95
  122.1 8.4 %conditional.6 = ((f32[8,4,128]{2,1,0:T(4,128)S(1)}, f32[8,4,128]{2,1,0:T(4,128)S(1)})) conditional(s32[]{:T(128)} %convert_element_type.205, (f32[8,4,128]{2,1,0:T(4,128)S(1)}, f32[8,4,128]{2,1,0:T(4,128)S(1)}) %tuple.175, (s32[2,8]{0,1:T(8,128)S(1)}, s32[]{:T(128)}, pred[]{:T(512)}, bf16[8,4096,256]{1,2,0:T(8,128)(2,1)}, ...), branch_computations={%region_4.4_spmd, %region_5.7_spmd} | conditional | flops 151265296 | bytes 24268952 | solution.py:89
  125.3 3.0 fusion.1
  128.3 2.1 select_reduce_fusion
  156.2 37.0 %while.52 = (s32[]{:T(128)}, f32[8,128,4,32]{1,3,2,0:T(8,128)}, s32[8]{0:T(128)S(1)}, s32[64,64]{0,1:T(8,128)}, s32[]{:T(128)}, /*index=5*/bf16[8,4096,256]{1,2,...) while((s32[]{:T(128)}, f32[8,128,4,32]{1,3,2,0:T(8,128)}, ...), condition=%wide.region_13.14_spmd, body=%wide.region_9.13_spmd.sunk | while | flops 277217376 | bytes 10375892 | solution.py:116
  159.5 10.1 %conditional.7 = (f32[8,128,4,32]{1,3,2,0:T(8,128)}) conditional(s32[]{:T(128)} %convert_element_type.206, f32[8,128,4,32]{1,3,2,0:T(8,128)} %get-tuple-element.1564, (s32[2,8]{0,1:T(8,128)S(1)}, s32[]{:T(128)}, pred[]{:T(512)}, bf16[8,4096,256]{1,2,0:T(8,128)(2,1)}, bf16[8,128,4,32]{1,3,2,0:T(8,128)(2,1)}, ...), branch_computations={%region_11.11_spmd, %region_12.12_spmd} | conditional | flops 277217312 | bytes 10375321 | solution.py:112
  159.5 3.3 constant_dynamic-slice_fusion.2
  164.8 4.8 fusion.14
  193.2 2.3 bitcast_reduce_fusion
  196.4 97.8 %while.53 = (s32[]{:T(128)}, f32[8,128,4,32]{1,3,2,0:T(8,128)}, bf16[8,512,4,128]{3,1,0,2:T(8,128)(2,1)}, bf16[8,512,8,128]{3,2,1,0:T(8,128)(2,1)}, s32[8]{0:T(1...) while((s32[]{:T(128)}, f32[8,128,4,32]{1,3,2,0:T(8,128)}, ...), condition=%wide.region_20.21_spmd, body=%wide.region_15.20_spmd.sunk | while | flops 2305949696 | bytes 124179344 | solution.py:180
  199.8 34.9 %conditional.8 = (f32[8,128,4,32]{1,3,2,0:T(8,128)}, bf16[1,512,4,128]{3,1,2,0:T(8,128)(2,1)}, bf16[1,512,8,128]{3,1,2,0:T(8,128)(2,1)S(1)}) conditional(s32[]{:T(128)} %convert_element_type.207, f32[8,128,4,32]{1,3,2,0:T(8,128)} %get-tuple-element.1617, (s32[2,8]{0,1:T(8,128)S(1)}, s32[]{:T(128)}, pred[]{:T(512)}, ...), branch_computations={%region_17.17_spmd, %region_18.19_spmd} | conditional | flops 2305949696 | bytes 121032976 | solution.py:178
  199.8 3.3 constant_dynamic-slice_fusion.4
  204.3 5.5 fusion.75
  210.0 6.9 fusion.73
  216.9 2.9 fusion.39
  223.4 3.7 fusion.29
  229.0 5.6 fusion.33
  266.6 2.0 bitcast_dynamic-update-slice_fusion.2
  282.6 1.9 bitcast_dynamic-update-slice_fusion.2
  290.5 2.0 bitcast_dynamic-update-slice_fusion.2
  294.8 412.0 %reduce-scatter.5.cloned.1.call-done = bf16[1024,4,128]{2,0,1:T(8,128)(2,1)} async-done(((bf16[4096,4,128]{2,0,1:T(8,128)(2,1)}), bf16[1024,4,128]{2,0,1:T(8,128)(2,1)}) %reduce-scatter.5.cloned.1.call-update) | async-done | bytes 1048592 | tf_op jit(solution)/shard_map/reduce_scatter | solution.py:199
  706.9 3.0 copy.118
  709.9 7.3 all-to-all-start
  723.2 2.0 convolution_convert_fusion.1
  725.2 8.8 %all-to-all-done = bf16[1024,4,128]{2,1,0:T(4,128)(2,1)S(1)} async-done(((bf16[1024,4,128]{2,1,0:T(4,128)(2,1)}), bf16[1024,4,128]{2,1,0:T(4,128)(2,1)S(1)}, u32[]{:S(2)}, u32[]{:S(2)}) %all-to-all-start) | async-done | bytes 1048608 | tf_op jit(solution)/shard_map/all_to_all | solution.py:202
  737.3 66.2 %reduce-scatter.3.cloned.1.call-done = bf16[128,8,128]{2,1,0:T(8,128)(2,1)} async-done(((bf16[4096,8,128]{2,1,0:T(8,128)(2,1)}), bf16[128,8,128]{2,1,0:T(8,128)(2,1)}) %reduce-scatter.3.cloned.1.call-update) | async-done | bytes 262160 | tf_op jit(solution)/shard_map/reduce_scatter | solution.py:185
  (215 shorter events, 124.0 us)
Async XLA Ops:
  7.2 186.1 %copy-start = (bf16[8,128,128]{2,1,0:T(8,128)(2,1)S(1)}, bf16[8,128,128]{2,1,0:T(8,128)(2,1)}, u32[]{:S(2)}) copy-start(bf16[8,128,128]{2,1,0:T(8,128)(2,1)} %param.23) | copy-start | bytes 786436
  7.2 14.0 %slice-start = ((bf16[128,512]{1,0:T(8,128)(2,1)}), bf16[128,256]{1,0:T(8,128)(2,1)S(1)}, s32[]{:S(2)}) async-start(bf16[128,512]{1,0:T(8,128)(2,1)} %param.21), calls=%async_computation.7 | async-start | bytes 131072
  7.2 61.5 %copy-start.10 = (bf16[128,512]{1,0:T(8,128)(2,1)S(1)}, bf16[128,512]{1,0:T(8,128)(2,1)}, u32[]{:S(2)}) copy-start(bf16[128,512]{1,0:T(8,128)(2,1)} %param.21) | copy-start | bytes 393220
  7.2 61.4 %all-gather.3.cloned.1.call-start = ((), (), s32[]{:S(2)}) async-start(), calls=%async_computation.3 | async-start | bytes 8650752 | tf_op jit(solution)/shard_map/all_gather | solution.py:51
  8.4 1.9 copy-start.13
  9.7 0.6 copy-start.18
  10.3 0.6 copy-start.16
  13.0 105.7 %all-gather.5.cloned.1.call-start = ((), (), s32[]{:S(2)}) async-start(), calls=%async_computation.4 | async-start | bytes 5242880 | tf_op jit(solution)/shard_map/all_gather | solution.py:50
  15.3 691.6 %reduce-scatter.5.cloned.1.call-start = ((), (), s32[]{:S(2)}) async-start(), calls=%async_computation.6 | async-start | bytes 5242880 | tf_op jit(solution)/shard_map/reduce_scatter | solution.py:199
  20.2 63.0 %copy-start.7 = (f32[1024,128]{1,0:T(8,128)}, f32[1024,128]{1,0:T(8,128)S(1)}, u32[]{:S(2)}) copy-start(f32[1024,128]{1,0:T(8,128)S(1)} %fusion.47) | copy-start | bytes 1572868
  199.8 10.2 %copy-start.20 = (f32[8,4,128]{2,1,0:T(4,128)S(1)}, f32[8,4,128]{2,1,0:T(4,128)}, u32[]{:S(2)}) copy-start(f32[8,4,128]{2,1,0:T(4,128)} %get-tuple-element.1016) | copy-start | bytes 49156 | tf_op jit(solution)/shard_map/while/body/eval_jaxpr/cond
  210.0 9.9 %copy-start.3 = (f32[8,4,512,128]{3,2,1,0:T(8,128)S(1)}, f32[8,4,512,128]{3,2,1,0:T(8,128)}, u32[]{:S(2)}) copy-start(f32[8,4,512,128]{3,2,1,0:T(8,128)} %fusion.75) | copy-start | bytes 25165828 | tf_op jit(solution)/shard_map/while/body/eval_jaxpr/cond
  210.0 9.8 %copy-start.12 = (bf16[8,128,4,32]{1,3,2,0:T(8,128)(2,1)S(1)}, bf16[8,128,4,32]{1,3,2,0:T(8,128)(2,1)}, u32[]{:S(2)}) copy-start(bf16[8,128,4,32]{1,3,2,0:T(8,128)(2,1)} %get-tuple-element.1017) | copy-start | bytes 786436 | tf_op jit(solution)/shard_map/while/body/eval_jaxpr/cond
  216.9 4.7 copy-start.2
  294.2 422.9 %copy-start.11 = (bf16[128,512]{1,0:T(8,128)(2,1)S(1)}, bf16[128,512]{1,0:T(8,128)(2,1)}, u32[]{:S(2)}) copy-start(bf16[128,512]{1,0:T(8,128)(2,1)} %param.21) | copy-start | bytes 393220
  294.2 425.4 %copy-start.5 = (f32[8,128,128]{1,2,0:T(8,128)S(1)}, f32[8,128,128]{1,2,0:T(8,128)}, u32[]{:S(2)}) copy-start(f32[8,128,128]{1,2,0:T(8,128)} %copy.106) | copy-start | bytes 1572868
  294.3 425.4 %copy-start.6 = (f32[8,128,128]{1,2,0:T(8,128)S(1)}, f32[8,128,128]{1,2,0:T(8,128)}, u32[]{:S(2)}) copy-start(f32[8,128,128]{1,2,0:T(8,128)} %get-tuple-element.1269) | copy-start | bytes 1572868
  294.3 509.2 %reduce-scatter.3.cloned.1.call-start = ((), (), s32[]{:S(2)}) async-start(), calls=%async_computation.5 | async-start | bytes 8650752 | tf_op jit(solution)/shard_map/reduce_scatter | solution.py:185
  294.3 428.9 %copy-start.8 = (f32[1024,128]{1,0:T(8,128)S(1)}, f32[1024,128]{1,0:T(8,128)}, u32[]{:S(2)}) copy-start(f32[1024,128]{1,0:T(8,128)} %copy-done.7) | copy-start | bytes 1572868
  294.3 428.9 %copy-start.15 = (bf16[128,128]{1,0:T(8,128)(2,1)S(1)}, bf16[128,128]{1,0:T(8,128)(2,1)}, u32[]{:S(2)}) copy-start(bf16[128,128]{1,0:T(8,128)(2,1)} %param.22) | copy-start | bytes 98308
  709.9 24.1 %all-to-all-start = ((bf16[1024,4,128]{2,1,0:T(4,128)(2,1)}), bf16[1024,4,128]{2,1,0:T(4,128)(2,1)S(1)}, u32[]{:S(2)}, u32[]{:S(2)}) async-start(bf16[1024,4,128]{2,1,0:T(4,128)(2,1)} %copy.118), calls=%async_computation.2 | async-start | bytes 2097152 | tf_op jit(solution)/shard_map/all_to_all | solution.py:202
  725.2 79.4 %copy-start.9 = (bf16[16,8,8,128]{3,1,2,0:T(8,128)(2,1)S(1)}, bf16[16,8,8,128]{3,1,2,0:T(8,128)(2,1)}, u32[]{:S(2)}) copy-start(bf16[16,8,8,128]{3,1,2,0:T(8,128)(2,1)} %copy.145) | copy-start | bytes 786436
  725.2 79.8 %copy-start.4 = (bf16[8,128,128]{2,1,0:T(8,128)(2,1)S(1)}, bf16[8,128,128]{2,1,0:T(8,128)(2,1)}, u32[]{:S(2)}) copy-start(bf16[8,128,128]{2,1,0:T(8,128)(2,1)} %param.18) | copy-start | bytes 786436
  725.2 79.8 %copy-start.14 = (f32[8,128]{1,0:T(8,128)S(1)}, f32[8,128]{1,0:T(8,128)}, u32[]{:S(2)}) copy-start(f32[8,128]{1,0:T(8,128)} %copy-done.13) | copy-start | bytes 12292
  734.1 71.3 %copy-start.19 = (f32[8,128]{1,0:T(8,128)S(1)}, f32[8,128]{1,0:T(8,128)}, u32[]{:S(2)}) copy-start(f32[8,128]{1,0:T(8,128)} %copy-done.18) | copy-start | bytes 12292
  734.1 71.3 %copy-start.17 = (f32[8,128]{1,0:T(8,128)S(1)}, f32[8,128]{1,0:T(8,128)}, u32[]{:S(2)}) copy-start(f32[8,128]{1,0:T(8,128)} %copy-done.16) | copy-start | bytes 12292
  734.1 73.3 %copy-start.1 = (bf16[8,128,128]{2,1,0:T(8,128)(2,1)S(1)}, bf16[8,128,128]{2,1,0:T(8,128)(2,1)}, u32[]{:S(2)}) copy-start(bf16[8,128,128]{2,1,0:T(8,128)(2,1)} %param.23) | copy-start | bytes 786436
Sparse Core Ops, SparseCore 0:
  13.1 55.5 all-gather.2
  70.9 47.7 all-gather.4
  294.4 412.4 reduce-scatter.4
  710.9 92.5 reduce-scatter.2
where the time goes:
time: 820 us; the launch traced here: 814 us
  waiting for transfers between devices  549 us (67%)
  local copies, waits for them, and re-layouts  103 us (13%)
  matrix products  55.8 us (7%)
  other arithmetic  51.1 us (6%)
  loops' own time  33.2 us (4%)
  between operations  14.1 us (2%)
    reduce_scatter x1, waiting for transfers between devices, on_device(): lax.psum_scatter(bias_terms.astype(jnp.bfloat16), 'row', scatter_dimensio...  412 us
    reduce_scatter x1, waiting for transfers between devices, on_device(): lax.psum_scatter(pair_terms.astype(jnp.bfloat16), 'col', scatter_dimensio...  66.2 us
    all_gather x1, waiting for transfers between devices, on_device(): gathered_slab = lax.all_gather(normed, 'col', axis=1, tiled=True)  47.3 us
    dynamic_update_slice x16, local copies, waits for them, and re-layouts, on_device(): lax.scan(grad_step, jnp.zeros((row_count, col_count, H, DH), jnp.float32)...  28.8 us
    while x4, local copies, waits for them, and re-layouts, on_device(): lax.scan(value_step, jnp.zeros((row_count, col_count, H, DH), jnp.float32...  24.8 us
  transfers between devices with their start and end apart: 5, of which 5 were waited for; matrix products, arithmetic and copies ran while one was open for 7% of the time, Pallas kernels for 0%

commit v1 on v0

--- a/solution.py
+++ b/solution.py
@@ -48,7 +48,9 @@
     gating = jax.nn.sigmoid(jnp.dot(flat_normed, w_gate, preferred_element_type=jnp.float32))
     gating = gating.reshape(row_count, col_count, head_width)
     bias_rows = lax.all_gather(pair_bias, "row", axis=2, tiled=True)
-    gathered_slab = lax.all_gather(normed, "col", axis=1, tiled=True)
+    gathered_slab = jnp.concatenate(
+        lax.all_to_all(jnp.stack([normed] * lax.axis_size("col")), "col", 0, 0), axis=1
+    )
     key_values = jnp.dot(
         gathered_slab.reshape(-1, channels), w_pair, preferred_element_type=jnp.float32
     )

time: 820 us -> 888 us (1.083)
  waiting for transfers between devices: 549 us -> 590 us
  local copies, waits for them, and re-layouts: 103 us -> 118 us
    all_to_all x0 -> x1, waiting for transfers between devices: none -> 109 us  [on_device(): lax.all_to_all(jnp.stack([normed] * lax.axis_size('col')), 'col', 0, 0)]
    all_gather x1 -> x0, waiting for transfers between devices: 47.3 us -> none  [on_device(): gathered_slab = lax.all_gather(normed, 'col', axis=1, tiled=True)]
    all_gather x1, waiting for transfers between devices: 14.2 us -> 0.01 us  [on_device(): bias_rows = lax.all_gather(pair_bias, 'row', axis=2, tiled=True)]
    all_to_all x0 -> x1, local copies, waits for them, and re-layouts: none -> 10.4 us  [on_device(): lax.all_to_all(jnp.stack([normed] * lax.axis_size('col')), 'col', 0, 0)]
  transfers between devices with their start and end apart: 5 -> 5, of which waited for: 5 -> 4; matrix products, arithmetic and copies ran while one was open for 7% -> 7% of each run, Pallas kernels for 0% -> 0%
where the time goes in v1:
time: 888 us; the launch traced here: 876 us
  waiting for transfers between devices  590 us (66%)
  local copies, waits for them, and re-layouts  118 us (13%)
  matrix products  53.1 us (6%)
  other arithmetic  50.5 us (6%)
  loops' own time  33.6 us (4%)
  starting transfers between devices  16 us (2%)
  between operations  14.4 us (2%)
    reduce_scatter x1, waiting for transfers between devices, on_device(): lax.psum_scatter(bias_terms.astype(jnp.bfloat16), 'row', scatter_dimensio...  405 us
    all_to_all x1, waiting for transfers between devices, on_device(): lax.all_to_all(jnp.stack([normed] * lax.axis_size('col')), 'col', 0, 0)  109 us
    reduce_scatter x1, waiting for transfers between devices, on_device(): lax.psum_scatter(pair_terms.astype(jnp.bfloat16), 'col', scatter_dimensio...  66.3 us
    dynamic_update_slice x16, local copies, waits for them, and re-layouts, on_device(): lax.scan(grad_step, jnp.zeros((row_count, col_count, H, DH), jnp.float32)...  29 us
    while x4, local copies, waits for them, and re-layouts, on_device(): lax.scan(value_step, jnp.zeros((row_count, col_count, H, DH), jnp.float32...  24.6 us
  transfers between devices with their start and end apart: 5, of which 4 were waited for; matrix products, arithmetic and copies ran while one was open for 7% of the time, Pallas kernels for 0%

profile of v1, /device:TPU:0, one launch (start us, length us, event | category | flops | bytes accessed | tf_op | source)
XLA Modules:
  0.0 875.5 jit_solution(18197724401220562661)
XLA Ops:
  12.2 5.4 stack.2
  17.6 8.7 all-to-all-start
  31.1 108.8 %all-to-all-done = bf16[32,8,128,128]{3,2,1,0:T(8,128)(2,1)} async-done(((bf16[32,8,128,128]{3,2,1,0:T(8,128)(2,1)}), bf16[32,8,128,128]{3,2,1,0:T(8,128)(2,1)}, u32[]{:S(2)}, u32[]{:S(2)}) %all-to-all-start) | async-done | bytes 8388640 | tf_op jit(solution)/shard_map/all_to_all | solution.py:52
  139.9 10.4 %copy.95 = bf16[32,8,128,128]{3,2,0,1:T(8,128)(2,1)} copy(bf16[32,8,128,128]{3,2,1,0:T(8,128)(2,1)} %all-to-all-done) | data formatting | bytes 16777216 | tf_op jit(solution)/shard_map/all_to_all | solution.py:52
  150.3 13.6 %convolution_convert_fusion = bf16[32768,256]{1,0:T(8,128)(2,1)} fusion(bf16[32768,128]{1,0:T(8,128)(2,1)} %bitcast.182, bf16[128,512]{1,0:T(8,128)(2,1)S(1)} %copy-done.11), kind=kOutput, calls=%fused_computation.54 | convolution fusion | flops 2155872256 | bytes 25231360 | tf_op jit(solution)/shard_map/dot_general | solution.py:54
  163.9 21.8 %copy.103 = bf16[8,4096,256]{1,2,0:T(8,128)(2,1)} copy(bf16[8,4096,256]{2,1,0:T(8,128)(2,1)} %bitcast.180) | data formatting | bytes 33554432 | tf_op jit(solution)/shard_map/while | solution.py:118
  185.8 36.3 %while.51 = (s32[]{:T(128)}, f32[8,4,128]{2,1,0:T(4,128)S(1)}, f32[8,4,128]{2,1,0:T(4,128)S(1)}, s32[8]{0:T(128)S(1)}, s32[64,64]{0,1:T(8,128)}, /*index=5*/s32[...) while((s32[]{:T(128)}, f32[8,4,128]{2,1,0:T(4,128)S(1)}, ...), condition=%wide.region_8.9_spmd, body=%wide.region_2.8_spmd.sunk | while | flops 151265344 | bytes 24269540 | solution.py:97
  189.2 8.4 conditional.6
  192.5 3.0 fusion.1
  195.4 2.1 select_reduce_fusion
  223.5 37.1 %while.52 = (s32[]{:T(128)}, f32[8,128,4,32]{1,3,2,0:T(8,128)}, s32[8]{0:T(128)S(1)}, s32[64,64]{0,1:T(8,128)}, s32[]{:T(128)}, /*index=5*/bf16[8,4096,256]{1,2,...) while((s32[]{:T(128)}, f32[8,128,4,32]{1,3,2,0:T(8,128)}, ...), condition=%wide.region_13.14_spmd, body=%wide.region_9.13_spmd.sunk | while | flops 277217376 | bytes 10375892 | solution.py:118
  226.8 10.1 %conditional.7 = (f32[8,128,4,32]{1,3,2,0:T(8,128)}) conditional(s32[]{:T(128)} %convert_element_type.206, f32[8,128,4,32]{1,3,2,0:T(8,128)} %get-tuple-element.1564, (s32[2,8]{0,1:T(8,128)S(1)}, s32[]{:T(128)}, pred[]{:T(512)}, bf16[8,4096,256]{1,2,0:T(8,128)(2,1)}, bf16[8,128,4,32]{1,3,2,0:T(8,128)(2,1)}, ...), branch_computations={%region_11.11_spmd, %region_12.12_spmd} | conditional | flops 277217312 | bytes 10375321 | solution.py:114
  226.9 3.3 constant_dynamic-slice_fusion.2
  232.2 4.8 fusion.14
  260.6 2.3 bitcast_reduce_fusion
  263.8 98.3 %while.53 = (s32[]{:T(128)}, f32[8,128,4,32]{1,3,2,0:T(8,128)}, bf16[8,512,4,128]{3,1,0,2:T(8,128)(2,1)}, bf16[8,512,8,128]{3,2,1,0:T(8,128)(2,1)}, s32[8]{0:T(1...) while((s32[]{:T(128)}, f32[8,128,4,32]{1,3,2,0:T(8,128)}, ...), condition=%wide.region_20.21_spmd, body=%wide.region_15.20_spmd.sunk | while | flops 2305949696 | bytes 124179344 | solution.py:182
  267.3 34.9 %conditional.8 = (f32[8,128,4,32]{1,3,2,0:T(8,128)}, bf16[1,512,4,128]{3,1,2,0:T(8,128)(2,1)}, bf16[1,512,8,128]{3,1,2,0:T(8,128)(2,1)S(1)}) conditional(s32[]{:T(128)} %convert_element_type.207, f32[8,128,4,32]{1,3,2,0:T(8,128)} %get-tuple-element.1617, (s32[2,8]{0,1:T(8,128)S(1)}, s32[]{:T(128)}, pred[]{:T(512)}, ...), branch_computations={%region_17.17_spmd, %region_18.19_spmd} | conditional | flops 2305949696 | bytes 121032976 | solution.py:180
  267.3 3.3 constant_dynamic-slice_fusion.4
  271.8 5.5 fusion.75
  277.5 6.9 fusion.73
  284.4 2.9 fusion.39
  291.0 3.7 fusion.29
  296.6 5.6 fusion.33
  326.2 2.0 bitcast_dynamic-update-slice_fusion.2
  334.3 2.0 bitcast_dynamic-update-slice_fusion.2
  350.3 2.0 bitcast_dynamic-update-slice_fusion.2
  362.9 405.2 %reduce-scatter.5.cloned.1.call-done = bf16[1024,4,128]{2,0,1:T(8,128)(2,1)} async-done(((bf16[4096,4,128]{2,0,1:T(8,128)(2,1)}), bf16[1024,4,128]{2,0,1:T(8,128)(2,1)}) %reduce-scatter.5.cloned.1.call-update) | async-done | bytes 1048592 | tf_op jit(solution)/shard_map/reduce_scatter | solution.py:201
  768.1 3.0 copy.119
  771.1 7.2 all-to-all-start.1
  784.5 2.0 convolution_convert_fusion.1
  786.4 8.7 all-to-all-done.1
  798.6 66.3 %reduce-scatter.3.cloned.1.call-done = bf16[128,8,128]{2,1,0:T(8,128)(2,1)} async-done(((bf16[4096,8,128]{2,1,0:T(8,128)(2,1)}), bf16[128,8,128]{2,1,0:T(8,128)(2,1)}) %reduce-scatter.3.cloned.1.call-update) | async-done | bytes 262160 | tf_op jit(solution)/shard_map/reduce_scatter | solution.py:187
  (220 shorter events, 124.4 us)
Async XLA Ops:
  7.2 253.4 %copy-start = (bf16[8,128,128]{2,1,0:T(8,128)(2,1)S(1)}, bf16[8,128,128]{2,1,0:T(8,128)(2,1)}, u32[]{:S(2)}) copy-start(bf16[8,128,128]{2,1,0:T(8,128)(2,1)} %param.23) | copy-start | bytes 786436
  8.3 1.9 copy-start.14
  9.7 0.6 copy-start.19
  10.3 0.6 copy-start.17
  17.5 8.8 %copy-start.10 = (bf16[4,128,1024]{2,1,0:T(8,128)(2,1)S(1)}, bf16[4,128,1024]{2,1,0:T(8,128)(2,1)}, u32[]{:S(2)}) copy-start(bf16[4,128,1024]{2,1,0:T(8,128)(2,1)} %param.19) | copy-start | bytes 3145732
  17.6 10.2 %copy-start.21 = (s32[64,64]{1,0:T(8,128)S(1)}, s32[64,64]{1,0:T(8,128)}, u32[]{:S(2)}) copy-start(s32[64,64]{1,0:T(8,128)} %param.20) | copy-start | bytes 49156
  17.6 10.9 %copy-start.11 = (bf16[128,512]{1,0:T(8,128)(2,1)S(1)}, bf16[128,512]{1,0:T(8,128)(2,1)}, u32[]{:S(2)}) copy-start(bf16[128,512]{1,0:T(8,128)(2,1)} %param.21) | copy-start | bytes 393220
  17.6 122.4 %all-to-all-start = ((bf16[32,8,128,128]{3,2,1,0:T(8,128)(2,1)}), bf16[32,8,128,128]{3,2,1,0:T(8,128)(2,1)}, u32[]{:S(2)}, u32[]{:S(2)}) async-start(bf16[32,8,128,128]{3,2,1,0:T(8,128)(2,1)} %stack.2), calls=%async_computation | async-start | bytes 16777216 | tf_op jit(solution)/shard_map/all_to_all | solution.py:52
  26.2 4.7 slice-start
  26.3 159.5 %all-gather.2.cloned.1.call-start = ((), (), s32[]{:S(2)}) async-start(), calls=%async_computation.4 | async-start | bytes 5242880 | tf_op jit(solution)/shard_map/all_gather | solution.py:50
  27.6 740.5 %reduce-scatter.5.cloned.1.call-start = ((), (), s32[]{:S(2)}) async-start(), calls=%async_computation.6 | async-start | bytes 5242880 | tf_op jit(solution)/shard_map/reduce_scatter | solution.py:201
  29.9 120.4 %copy-start.7 = (f32[1024,128]{1,0:T(8,128)}, f32[1024,128]{1,0:T(8,128)S(1)}, u32[]{:S(2)}) copy-start(f32[1024,128]{1,0:T(8,128)S(1)} %fusion.47) | copy-start | bytes 1572868
  267.3 10.2 %copy-start.22 = (f32[8,4,128]{2,1,0:T(4,128)S(1)}, f32[8,4,128]{2,1,0:T(4,128)}, u32[]{:S(2)}) copy-start(f32[8,4,128]{2,1,0:T(4,128)} %get-tuple-element.1016) | copy-start | bytes 49156 | tf_op jit(solution)/shard_map/while/body/eval_jaxpr/cond
  277.5 9.9 %copy-start.3 = (f32[8,4,512,128]{3,2,1,0:T(8,128)S(1)}, f32[8,4,512,128]{3,2,1,0:T(8,128)}, u32[]{:S(2)}) copy-start(f32[8,4,512,128]{3,2,1,0:T(8,128)} %fusion.75) | copy-start | bytes 25165828 | tf_op jit(solution)/shard_map/while/body/eval_jaxpr/cond
  277.5 9.9 %copy-start.13 = (bf16[8,128,4,32]{1,3,2,0:T(8,128)(2,1)S(1)}, bf16[8,128,4,32]{1,3,2,0:T(8,128)(2,1)}, u32[]{:S(2)}) copy-start(bf16[8,128,4,32]{1,3,2,0:T(8,128)(2,1)} %get-tuple-element.1017) | copy-start | bytes 786436 | tf_op jit(solution)/shard_map/while/body/eval_jaxpr/cond
  284.4 4.7 copy-start.2
  362.1 416.2 %copy-start.12 = (bf16[128,512]{1,0:T(8,128)(2,1)S(1)}, bf16[128,512]{1,0:T(8,128)(2,1)}, u32[]{:S(2)}) copy-start(bf16[128,512]{1,0:T(8,128)(2,1)} %param.21) | copy-start | bytes 393220
  362.2 418.7 %copy-start.5 = (f32[8,128,128]{1,2,0:T(8,128)S(1)}, f32[8,128,128]{1,2,0:T(8,128)}, u32[]{:S(2)}) copy-start(f32[8,128,128]{1,2,0:T(8,128)} %copy.107) | copy-start | bytes 1572868
  362.2 418.7 %copy-start.6 = (f32[8,128,128]{1,2,0:T(8,128)S(1)}, f32[8,128,128]{1,2,0:T(8,128)}, u32[]{:S(2)}) copy-start(f32[8,128,128]{1,2,0:T(8,128)} %get-tuple-element.1269) | copy-start | bytes 1572868
  362.2 502.7 %reduce-scatter.3.cloned.1.call-start = ((), (), s32[]{:S(2)}) async-start(), calls=%async_computation.5 | async-start | bytes 8650752 | tf_op jit(solution)/shard_map/reduce_scatter | solution.py:187
  362.2 422.2 %copy-start.8 = (f32[1024,128]{1,0:T(8,128)S(1)}, f32[1024,128]{1,0:T(8,128)}, u32[]{:S(2)}) copy-start(f32[1024,128]{1,0:T(8,128)} %copy-done.7) | copy-start | bytes 1572868
  362.3 422.2 %copy-start.16 = (bf16[128,128]{1,0:T(8,128)(2,1)S(1)}, bf16[128,128]{1,0:T(8,128)(2,1)}, u32[]{:S(2)}) copy-start(bf16[128,128]{1,0:T(8,128)(2,1)} %param.22) | copy-start | bytes 98308
  771.1 24.1 %all-to-all-start.1 = ((bf16[1024,4,128]{2,1,0:T(4,128)(2,1)}), bf16[1024,4,128]{2,1,0:T(4,128)(2,1)S(1)}, u32[]{:S(2)}, u32[]{:S(2)}) async-start(bf16[1024,4,128]{2,1,0:T(4,128)(2,1)} %copy.119), calls=%async_computation.3 | async-start | bytes 2097152 | tf_op jit(solution)/shard_map/all_to_all | solution.py:204
  786.4 79.6 %copy-start.9 = (bf16[16,8,8,128]{3,1,2,0:T(8,128)(2,1)S(1)}, bf16[16,8,8,128]{3,1,2,0:T(8,128)(2,1)}, u32[]{:S(2)}) copy-start(bf16[16,8,8,128]{3,1,2,0:T(8,128)(2,1)} %copy.146) | copy-start | bytes 786436
  786.4 79.9 %copy-start.4 = (bf16[8,128,128]{2,1,0:T(8,128)(2,1)S(1)}, bf16[8,128,128]{2,1,0:T(8,128)(2,1)}, u32[]{:S(2)}) copy-start(bf16[8,128,128]{2,1,0:T(8,128)(2,1)} %param.18) | copy-start | bytes 786436
  786.4 79.9 %copy-start.15 = (f32[8,128]{1,0:T(8,128)S(1)}, f32[8,128]{1,0:T(8,128)}, u32[]{:S(2)}) copy-start(f32[8,128]{1,0:T(8,128)} %copy-done.14) | copy-start | bytes 12292
  795.3 71.5 %copy-start.20 = (f32[8,128]{1,0:T(8,128)S(1)}, f32[8,128]{1,0:T(8,128)}, u32[]{:S(2)}) copy-start(f32[8,128]{1,0:T(8,128)} %copy-done.19) | copy-start | bytes 12292
  795.3 71.5 %copy-start.18 = (f32[8,128]{1,0:T(8,128)S(1)}, f32[8,128]{1,0:T(8,128)}, u32[]{:S(2)}) copy-start(f32[8,128]{1,0:T(8,128)} %copy-done.17) | copy-start | bytes 12292
  795.3 73.4 %copy-start.1 = (bf16[8,128,128]{2,1,0:T(8,128)(2,1)S(1)}, bf16[8,128,128]{2,1,0:T(8,128)(2,1)}, u32[]{:S(2)}) copy-start(bf16[8,128,128]{2,1,0:T(8,128)(2,1)} %param.23) | copy-start | bytes 786436
Sparse Core Ops, SparseCore 0:
  29.3 49.5 all-gather.1
  362.3 405.7 reduce-scatter.4
  772.3 92.5 reduce-scatter.2
